TPU v7x, 32 devices: a whole 2x2x4 slice. The times are simulated.
32 devices in a mesh: domain: 8 (over z, x), group: 4 (over y, core).
Axes of the slice: x: 2, y: 2, z: 4, core: 2. Of those that a mesh axis runs over, the one named last changes fastest.
Arguments:
- centers: float32 [2048, 3], P(('domain', 'group')), may hold values from -24 to 24
- offsets: float32 [2048, 3, 144], P(('domain', 'group')), may hold values from -6 to 6
- density: float32 [2048, 3, 144], P(('domain', 'group')), may hold values from -6 to 6
- area: float32 [2048, 144], P(('domain', 'group')), may hold values from 0.03 to 0.3
- upsample: float32 [544, 144], replicated
- self_operator: float32 [144, 144], replicated, may hold values from -0.5 to 0.5
- near_sources: int32 [2048, 4], P(('domain', 'group')), may hold values from 0 to 2047, as said below
- near_counts: int32 [2048], P(('domain', 'group')), may hold values from 1 to 4, as said below
- leaf_slot: int32 [2048], P(('domain', 'group')), may hold values from 0 to 4095, as said below
- leaf_list: int32 [256, 8], P(('domain', 'group')), may hold values from 0 to 255
Outputs:
- velocity: float32 [2048, 3, 144], P(('domain', 'group'))
Inputs may be any that keep to these rules, and one draw needn't show every extreme that they name: `near_sources`: each near source lies in the target's own domain or in one of the two adjacent domains of 2048 / 8 vesicles, and is never the target itself; slots past the count hold valid indices too. `near_counts`: the first vesicle of every device has 4 live slots. `leaf_slot`: no two vesicles share a slot, and a vesicle's slot lies in a leaf block of a device of its own domain.
All inputs are finite; a program needn't handle non-finite values.
Results may differ from a plain program's by a relative error of at most 0.00014.
Values sent between devices are 32-bit elements; how exact they have to be, the bound alone decides.
No kernel may reach another device: no remote copies, remote signals or barrier semaphores. Data moves between devices by JAX's collectives and lax.ppermute only.
A program may use at most 128 MiB of HBM per device.

v0:
```python
import functools

import jax
import jax.numpy as jnp
from jax import lax
from jax.experimental import pallas as pl
from jax.experimental.pallas import tpu as pltpu
from jax.sharding import PartitionSpec as P

LEAF_CAP = 16
EPS = 0.5
UNITS = 8
BATCH = 32
TAILS = 16
PADS = BATCH + 2 * UNITS
HALF = 48
F32 = jnp.float32
BF16 = jnp.bfloat16
HIGHEST = lax.Precision.HIGHEST
VMEM_SPEC = pl.BlockSpec(memory_space=pltpu.VMEM)
SMEM_SPEC = pl.BlockSpec(memory_space=pltpu.SMEM)


def params(mib=60):
    return pltpu.CompilerParams(vmem_limit_bytes=mib << 20)


def cost(micros):
    return pl.CostEstimate(
        flops=int(micros * 1e9), bytes_accessed=int(micros * 3e6), transcendentals=0
    )


def iota(shape, dim):
    return lax.broadcasted_iota(jnp.int32, shape, dim)


def split3(value):
    high = value.astype(BF16).astype(F32)
    rest = value - high
    mid = rest.astype(BF16).astype(F32)
    return high, mid, rest - mid


def stack_left(value, axis):
    h, m, l = split3(value)
    return jnp.concatenate([h, m, l, h, m, h], axis=axis)


def stack_right(value, axis):
    h, m, l = split3(value)
    return jnp.concatenate([h, h, h, m, m, l], axis=axis)


def dot_nt(a, b, precision=None):
    return lax.dot_general(
        a, b, (((1,), (1,)), ((), ())), precision=precision, preferred_element_type=F32
    )


def column(row):
    n = row.shape[1]
    eye = iota((n, n), 0) == iota((n, n), 1)
    return jnp.sum(jnp.where(eye, row, jnp.zeros_like(row)), axis=1, keepdims=True)


def as_row(col):
    n = col.shape[0]
    eye = iota((n, n), 0) == iota((n, n), 1)
    return jnp.sum(jnp.where(eye, col, jnp.zeros_like(col)), axis=0, keepdims=True)


def pack_kernel(cen_ref, off_ref, den_ref, area_ref, leaf_ref, list_ref, tile_ref):
    rows, points = area_ref.shape
    area = area_ref[...]
    tail = points - 128
    tails = []
    lines = []
    for c in range(3):
        grid = off_ref[c] + column(cen_ref[c : c + 1, :])
        tile_ref[pl.ds(c, rows, 8), :] = grid[:, :128]
        tails.append(grid[:, 128:])
    tails.append(jnp.zeros((rows, tail), F32))
    for c in range(3):
        weighted = den_ref[c] * area
        tile_ref[pl.ds(4 + c, rows, 8), :] = weighted[:, :128]
        tails.append(weighted[:, 128:])
        lines.append(as_row(jnp.sum(weighted, axis=1, keepdims=True)))
    tails.append(jnp.zeros((rows, tail), F32))
    tile_ref[pl.ds(3, rows, 8), :] = jnp.concatenate(tails, axis=1)
    tile_ref[pl.ds(7, rows, 8), :] = jnp.zeros((rows, 128), F32)
    leaf = (leaf_ref[...] // LEAF_CAP).astype(F32)
    block = jnp.concatenate([cen_ref[...]] + lines + [leaf, jnp.zeros((1, rows), F32)], axis=0)
    lists = list_ref[...].astype(F32)
    rest = 128 - rows - lists.shape[1]
    tile_ref[8 * rows :, :] = jnp.concatenate([block, lists, jnp.zeros((8, rest), F32)], axis=1)


def pack(cen, off, den, area, leaf, lists):
    rows = area.shape[0]
    return pl.pallas_call(
        pack_kernel,
        out_shape=jax.ShapeDtypeStruct((8 * rows + 8, 128), F32),
        in_specs=[VMEM_SPEC] * 6,
        out_specs=VMEM_SPEC,
        compiler_params=params(),
        cost_estimate=cost(2),
        name="pack",
    )(cen, off, den, area, leaf, lists)


def quotient(value, by):
    if by & (by - 1) == 0:
        return lax.shift_right_logical(value, by.bit_length() - 1), jnp.bitwise_and(value, by - 1)
    return lax.div(value, by), lax.rem(value, by)


def encode(spot, slot, target):
    return spot * (1 << 12) + slot * (1 << 8) + target


def target_of(code):
    return jnp.bitwise_and(code, (1 << 8) - 1)


def slot_of(code):
    return jnp.bitwise_and(lax.shift_right_logical(code, 8), 15)


def spot_of(code):
    return lax.shift_right_logical(code, 12)


def add_pairs(groups, src_ref, cnt_ref, list_ref, t, ends):
    slots, rows = src_ref.shape
    domain = lax.axis_index("domain")
    group = lax.axis_index("group")
    live = cnt_ref[0, t]
    ends = list(ends)
    for k in range(slots):
        device, local = quotient(src_ref[k, t], rows)
        home, turn = quotient(device, groups)
        step = home - domain
        here = step == 0
        held = jnp.where(here, rows, 2 * rows)
        spot = jnp.bitwise_xor(turn, group) * held + local + jnp.where(step > 0, rows, 0)
        list_ref[jnp.where(here, 0, 1), jnp.where(here, ends[0], ends[1])] = encode(spot, k, t)
        is_live = k < live
        ends[0] += jnp.where(jnp.logical_and(is_live, here), 1, 0)
        ends[1] += jnp.where(jnp.logical_and(is_live, jnp.logical_not(here)), 1, 0)
    return tuple(ends)


def end_lists(block, list_ref, ends):
    width = list_ref.shape[1]
    for which in range(2):
        list_ref[which, width - 1] = ends[which]
        for i in range(PADS):
            list_ref[which, ends[which] + i] = encode((which + 1) * block, 0, 0)


def setup_kernel(den_ref, op_ref, up_ref, self_ref, upw_ref):
    points = den_ref.shape[2]
    for c in range(3):
        self_ref[c] = dot_nt(den_ref[c], op_ref[...], HIGHEST)

    fine = up_ref.shape[1]
    full = fine // 128 * 128
    rest = fine - full
    tail = points - 128
    up = up_ref[...]
    wide = jnp.concatenate([up[:, :full]] + [up[:, full:]] * (128 // rest), axis=1)
    spare = jnp.zeros((128 - 6 * tail, full + 128), F32)
    upw_ref[...] = jnp.concatenate(
        [stack_right(wide[:128], 0), stack_right(wide[128:], 0), spare], axis=0
    ).astype(BF16)


def setup(den, op, up_t):
    fine = up_t.shape[1]
    return pl.pallas_call(
        setup_kernel,
        out_shape=(
            jax.ShapeDtypeStruct(den.shape, F32),
            jax.ShapeDtypeStruct((6 * 128 + 128, fine // 128 * 128 + 128), BF16),
        ),
        in_specs=[VMEM_SPEC] * 3,
        out_specs=(VMEM_SPEC,) * 2,
        compiler_params=params(24),
        cost_estimate=cost(5),
        name="setup",
    )(den, op, up_t)


def left_kernel(groups, src_ref, cnt_ref, off_ref, left_ref, list_ref):
    _, rows, points = off_ref.shape
    eye = (iota((points, points), 0) == iota((points, points), 1)).astype(BF16)

    def one_left(t):
        x = [off_ref[c, pl.ds(t, 1), :] * (1.0 / EPS) for c in range(3)]
        xx = x[0] * x[0] + x[1] * x[1] + x[2] * x[2]
        one = jnp.ones_like(xx)
        zero = jnp.zeros_like(xx)
        cases = [x + [one, xx, zero, zero, zero]]
        for c in range(3):
            extra = [x[c] * x[b] for b in range(3)]
            extra[c] = extra[c] + xx
            cases.append(x + [one] + extra + [zero])
        stacked = [stack_left(jnp.concatenate(v, axis=0), 0) for v in cases]
        for p in range(2):
            both = jnp.concatenate(stacked[2 * p : 2 * p + 2], axis=0).astype(BF16)
            left_ref[t, p, :, : 2 * HALF] = dot_nt(eye, both).astype(BF16)

    each = 8

    def some_left(i, ends):
        for j in range(each):
            ends = add_pairs(groups, src_ref, cnt_ref, list_ref, i * each + j, ends)
            one_left(i * each + j)
        return ends

    ends = lax.fori_loop(0, rows // each, some_left, (0, 0))
    end_lists(groups * rows, list_ref, ends)


def left(groups, src, cnt, off):
    _, rows, points = off.shape
    return pl.pallas_call(
        functools.partial(left_kernel, groups),
        out_shape=(
            jax.ShapeDtypeStruct((rows, 2, points, 128), BF16),
            jax.ShapeDtypeStruct((2, src.shape[0] * rows + PADS + 1), jnp.int32),
        ),
        in_specs=[SMEM_SPEC] * 2 + [VMEM_SPEC],
        out_specs=(VMEM_SPEC, SMEM_SPEC),
        compiler_params=params(24),
        cost_estimate=cost(10),
        name="left",
    )(src, cnt, off)


def right(ref):
    tile = ref[...]
    sub = iota(tile.shape, 0)
    y = [ref[c : c + 1, :] for c in range(3)]
    f = [ref[4 + c : 5 + c, :] for c in range(3)]
    yy = y[0] * y[0] + y[1] * y[1] + y[2] * y[2]
    yf = y[0] * f[0] + y[1] * f[1] + y[2] * f[2]
    rest = jnp.where(sub < 4, 0.0, tile)
    points = jnp.where(sub < 3, -2.0 * tile, jnp.where(sub == 3, yy + 2.0, 0.0))
    forces = jnp.where(sub < 3, -pltpu.roll(tile, 4, 0), jnp.where(sub == 3, yf, 0.0))
    outs = [points + jnp.where(sub == 3, -1.0, jnp.where(sub == 4, 1.0, 0.0))]
    for c in range(3):
        outs.append(f[c] * points + y[c] * forces + jnp.where(sub == c, -yf, rest))
    return [stack_right(v, 0).astype(BF16) for v in outs]


def shifted(tile, center):
    sub = iota(tile.shape, 0)
    shift = jnp.where(sub == 0, center[0], jnp.where(sub == 1, center[1], center[2]))
    return jnp.where(sub < 3, (tile - shift) * (1.0 / EPS), tile)


def place_right(w, parts):
    width = parts[0].shape[1]
    for o, part in enumerate(parts):
        h = o % 2
        w[o // 2, h * HALF : (h + 1) * HALF, h * width : (h + 1) * width] = part


def evaluate(lefts, w, width):
    sums = [0.0, 0.0, 0.0]
    total = w.shape[2] // 2
    for start in range(0, total, width):
        if width == total:
            wide = [
                jnp.dot(lefts[p], w[p], preferred_element_type=F32) for p in range(2)
            ]
            found = [v[:, h * width : (h + 1) * width] for v in wide for h in range(2)]
        else:
            found = [
                jnp.dot(
                    lefts[o // 2],
                    w[o // 2, :, o % 2 * total + start : o % 2 * total + start + width],
                    preferred_element_type=F32,
                )
                for o in range(4)
            ]
        u = lax.rsqrt(found[0])
        cube = u * u * u
        for c in range(3):
            product = cube * found[1 + c]
            for j in range(0, width, 128):
                sums[c] = sums[c] + product[:, j : j + 128]
    return [jnp.sum(s, axis=1, keepdims=True) for s in sums]


def near_kernel(n_blocks, which, last, groups, n_far, slots, *refs):
    list_ref, cen_ref = refs[:2]
    blocks = refs[2 : 2 + n_blocks]
    refs = refs[2 + n_blocks :]
    left_ref, upw_ref = refs[:2]
    refs = refs[2:]
    if last:
        cols_in, tail_in, self_ref = refs[:3]
        far_refs = refs[3 : 3 + n_far]
        out_ref = refs[3 + n_far]
        pool, fine, tails, cols, wa, wb, wt = refs[4 + n_far :]
    else:
        cols, tails, pool, fine, wa, wb = refs

    rows = left_ref.shape[0]
    points = left_ref.shape[2]
    full = upw_ref.shape[1] - 128
    held = blocks[0].shape[0] // rows * rows
    for i, block in enumerate(blocks):
        pool[pl.ds(i * held, held)] = block[:held]
    pool[n_blocks * held] = jnp.zeros((8, 128), F32)
    wa[...] = jnp.zeros_like(wa)
    wb[...] = jnp.zeros_like(wb)
    if last:
        wt[...] = jnp.zeros_like(wt)
        cols[...] = cols_in[...]
        tails[...] = tail_in[...]
    else:
        cols[...] = jnp.zeros_like(cols)
        tails[...] = jnp.zeros_like(tails)

    n = list_ref[which, list_ref.shape[1] - 1]
    sub = iota((8, 128), 0)
    lane = iota((8, 128), 1)
    body = sub % 4 < 3
    tail = points - 128
    own_lanes = jnp.logical_and(lane // tail == sub, body)
    part = iota((8 * BATCH, 128), 1) // tail
    k_lane = lane // (128 // slots)

    def center_of(t):
        return [cen_ref[c, t] for c in range(3)]

    def upsample(b, _):
        tiles = [pool[spot_of(list_ref[which, b * BATCH + j])] for j in range(BATCH)]
        heads = jnp.concatenate([jnp.where(body, v, 0.0) for v in tiles], axis=0)
        ends = jnp.concatenate([jnp.where(own_lanes, v[3:4, :], 0.0) for v in tiles], axis=0)
        reach = tail
        while reach < 128:
            ends = ends + pltpu.roll(ends, reach, 1)
            reach *= 2
        h, m, l = split3(ends)
        ends = jnp.where(part == 2, l, jnp.where(jnp.logical_or(part == 1, part == 4), m, h))
        wide = jnp.concatenate([stack_left(heads, 1), ends], axis=1).astype(BF16)
        out = jnp.dot(wide, upw_ref[...], preferred_element_type=F32)
        out = out.reshape(BATCH, 8, full + 128)
        for j in range(BATCH):
            i = b * BATCH + j
            code = list_ref[which, i]
            t = target_of(code)
            center = center_of(t)
            fine[i] = shifted(out[j, :, :full], center)
            mine = jnp.logical_and(k_lane == slot_of(code), i < n)
            tails[t] = jnp.where(mine, shifted(out[j, :, full:], center), tails[t])
        return 0

    lax.fori_loop(0, (n + BATCH - 1) // BATCH, upsample, 0)

    lane_p = iota((points, 128), 1)

    def add_cols(found):
        for c in range(3):
            value = cols[c]
            for t, sums in found:
                value = value + jnp.where(lane_p == t, sums[c], 0.0)
            cols[c] = value

    def build(i, w):
        for j in range(UNITS):
            place_right(w.at[j], right(fine.at[i * UNITS + j]))

    def main(i, w):
        found = []
        for j in range(UNITS):
            t = target_of(list_ref[which, i * UNITS + j])
            lefts = [left_ref[t, p, :, : 2 * HALF] for p in range(2)]
            found.append((t, evaluate(lefts, w.at[j], 256)))
        add_cols(found)

    build(0, wa)

    def two(i, _):
        build(2 * i + 1, wb)
        main(2 * i, wa)
        build(2 * i + 2, wa)
        main(2 * i + 1, wb)
        return 0

    lax.fori_loop(0, (n + 2 * UNITS - 1) // (2 * UNITS), two, 0)

    if last:

        def tail_pass(i, _):
            found = []
            for j in range(TAILS):
                t = i * TAILS + j
                place_right(wt.at[j], right(tails.at[t]))
                lefts = [left_ref[t, p, :, : 2 * HALF] for p in range(2)]
                found.append((t, evaluate(lefts, wt.at[j], 128)))
            for c in range(3):
                value = jnp.zeros((points, 128), F32)
                for t, sums in found:
                    value = jnp.where(lane_p == t, sums[c], value)
                cols[c] += value
            return 0

        lax.fori_loop(0, rows // TAILS, tail_pass, 0)
        far = far_sums(groups, rows, far_refs)
        for c in range(3):
            turned = jnp.transpose(cols[c])[:rows]
            out_ref[c] = turned * (1.0 / EPS) + self_ref[c] + far[c]


def near(which, last, groups, blocks, lists, cen, lefts, upw, extra, far=()):
    rows, _, points, _ = lefts.shape
    full = upw.shape[1] - 128
    n_blocks = len(blocks)
    size = lists.shape[1] - 1
    slots = (size - PADS) // rows
    cols = jax.ShapeDtypeStruct((3, points, 128), F32)
    tails = jax.ShapeDtypeStruct((rows, 8, 128), F32)
    if last:
        out_shape = jax.ShapeDtypeStruct((3, rows, points), F32)
        out_specs = VMEM_SPEC
    else:
        out_shape = (cols, tails)
        out_specs = (VMEM_SPEC, VMEM_SPEC)
    scratch = [
        pltpu.VMEM((n_blocks * (blocks[0].shape[0] // rows * rows) + 1, 8, 128), F32),
        pltpu.VMEM((size, 8, full), F32),
    ]
    if last:
        scratch += [pltpu.VMEM(tails.shape, F32), pltpu.VMEM(cols.shape, F32)]
    scratch += [pltpu.VMEM((UNITS, 2, 2 * HALF, 2 * full), BF16)] * 2
    if last:
        scratch += [pltpu.VMEM((TAILS, 2, 2 * HALF, 256), BF16)]
    n_vmem = n_blocks + 2 + len(extra) + len(far)
    return pl.pallas_call(
        functools.partial(near_kernel, n_blocks, which, last, groups, len(far), slots),
        out_shape=out_shape,
        in_specs=[SMEM_SPEC] * 2 + [VMEM_SPEC] * n_vmem,
        out_specs=out_specs,
        scratch_shapes=scratch,
        compiler_params=params(44),
        cost_estimate=cost(25 if last else 0.3),
        name="near_last" if last else "near_own",
    )(lists, cen, *blocks, lefts, upw, *extra, *far)


def far_sums(groups, rows, refs):
    domain = lax.axis_index("domain")
    group = lax.axis_index("group")
    block = refs[0][0][:, :rows]
    center = [column(block[c : c + 1]) for c in range(3)]
    leaf = column(block[6:7])
    leaves = jnp.concatenate(
        [refs[0][jnp.bitwise_xor(group, g)][:, rows : rows + 8] for g in range(groups)], axis=0
    )
    count = groups * 8
    first = (domain * count).astype(F32)
    hot = (leaf - first == iota((rows, count), 1).astype(F32)).astype(F32)
    lists = jnp.dot(hot, leaves, precision=HIGHEST, preferred_element_type=F32)
    lists = jnp.round(lists)
    wanted = [jnp.broadcast_to(lists[:, k : k + 1], (rows, 128)) for k in range(8)]
    lane = iota((8, 128), 1)

    def one(ref, i, sums):
        both = jnp.where(lane < rows, ref[2 * i], pltpu.roll(ref[2 * i + 1], rows, 1))
        rel = [center[c] - both[c : c + 1] for c in range(3)]
        force = [both[3 + c : 4 + c] for c in range(3)]
        source = both[6:7]
        times = jnp.zeros((rows, 128), F32)
        for k in range(8):
            times = times + jnp.where(wanted[k] == source, 1.0, 0.0)
        dist = rel[0] * rel[0] + rel[1] * rel[1] + rel[2] * rel[2] + EPS * EPS
        u = lax.rsqrt(dist)
        u3 = u * u * u * times
        near_part = (dist + EPS * EPS) * u3
        project = (rel[0] * force[0] + rel[1] * force[1] + rel[2] * force[2]) * u3
        return [sums[c] + near_part * force[c] + project * rel[c] for c in range(3)]

    sums = [jnp.zeros((rows, 128), F32)] * 3
    for ref in refs:
        sums = lax.fori_loop(0, ref.shape[0] // 2, functools.partial(one, ref), sums, unroll=min(4, ref.shape[0] // 2))
    return [jnp.sum(v, axis=1, keepdims=True) for v in sums]


def swap(x, axis, bit):
    return lax.ppermute(x, axis, [(i, i ^ bit) for i in range(lax.axis_size(axis))])


def bits(n):
    found = []
    bit = 1
    while bit < n:
        found.append(bit)
        bit *= 2
    return found


def shards(
    centers,
    offsets,
    density,
    area,
    upsample,
    self_operator,
    near_sources,
    near_counts,
    leaf_slot,
    leaf_list,
):
    rows = centers.shape[0]
    groups = lax.axis_size("group")
    domains = lax.axis_size("domain")
    cen = centers.T
    off = jnp.transpose(offsets, (1, 0, 2))
    den = jnp.transpose(density, (1, 0, 2))
    tiles = pack(cen, off, den, area, leaf_slot[None, :], leaf_list)
    tiles = tiles.reshape(rows + 1, 8, 128)
    ends = domains - 1
    above = lax.ppermute(tiles, "domain", [(i + 1, i) for i in range(ends)])
    below = lax.ppermute(tiles, "domain", [(i, i + 1) for i in range(ends)])
    own = by_group(tiles, groups)

    lefts, lists = left(groups, near_sources.T, near_counts[None, :], off)
    own, below, above, den = after((own, below, above, den), (lefts,))
    both = jnp.concatenate([below[:rows], above[:rows]], axis=0)
    far = [jnp.concatenate([v[rows:] for v in own], axis=0)]
    hops = []
    steps = bits(domains)
    self_term = None
    for turn in range(max(len(steps), groups - 1)):
        if turn < len(steps):
            far.append(swap(jnp.concatenate(far, axis=0), "domain", steps[turn]))
        if turn + 1 < groups:
            hops.append(swap(both, "group", turn + 1))
        if turn == 0:
            self_term, upw = setup(den, self_operator, upsample.T)
            far = after(far, (self_term,))
    sides = [both] + hops
    lists = after(lists, far[:-1])
    cols, tails = near(0, False, groups, own, lists, cen, lefts, upw, ())
    out = near(
        1, True, groups, sides, lists, cen, lefts, upw, (cols, tails, self_term), far
    )
    return jnp.transpose(out, (1, 0, 2))


def after(values, others):
    return lax.optimization_barrier((values, others))[0]


def by_group(block, groups):
    return [block] + [swap(block, "group", i) for i in range(1, groups)]


def combine(held, steps):
    whole = held[0] if len(held) == 1 else jnp.concatenate(held, axis=0)
    masks = [steps[0]] if len(steps) == 1 else [steps[0], steps[1], steps[0] ^ steps[1]]
    return [swap(whole, "domain", mask) for mask in masks]


def solution(mesh):
    in_specs = (
        P(("domain", "group"), None),
        P(("domain", "group"), None, None),
        P(("domain", "group"), None, None),
        P(("domain", "group"), None),
        P(),
        P(),
        P(("domain", "group"), None),
        P(("domain", "group")),
        P(("domain", "group")),
        P(("domain", "group"), None),
    )
    out_specs = P(("domain", "group"), None, None)
    return jax.shard_map(shards, mesh=mesh, in_specs=in_specs, out_specs=out_specs, check_vma=False)
```

profile of v0, /device:TPU:0, one launch (start us, length us, event | category | flops | bytes accessed | tf_op | source)
XLA Modules:
  0.0 84.7 jit_solution(3644369782905002639)
XLA Ops:
  0.0 0.0 copy-start.3
  0.0 0.0 copy-start.6
  0.0 0.0 copy-start.7
  0.0 2.0 %pack.1 = f32[520,128]{1,0:T(8,128)} custom-call(f32[3,64]{1,0:T(4,128)} %bitcast.16, f32[3,64,144]{2,1,0:T(8,128)} %bitcast.20, f32[3,64,144]{2,1,0:T(8,128)} %bitcast.22, f32[64,144]{1,0:T(8,128)} %area_ref.1, s32[1,64]{1,0:T(1,128)} %bitcast.26, s32[8,8]{1,0:T(8,128)} %list_ref.1), custom_call_target="tpu_custom_call" | custom-call | flops 2000000000 | bytes 6000000 | tf_op jit(solution)/shard_map/pack/pallas_call | solution.py:101
  2.0 0.5 collective-permute-start
  2.5 2.5 %collective-permute-start.1 = (f32[65,8,128]{2,1,0:T(8,128)}, f32[65,8,128]{2,1,0:T(8,128)S(1)}, u32[]{:S(2)}, u32[]{:S(2)}) collective-permute-start(f32[65,8,128]{2,1,0:T(8,128)} %bitcast.10), channel_id=1, source_target_pairs={{0,2},{1,3},{2,0},{3,1},{4,6},{5,7},{6,4},{7,5},{8,10},{9,11},{10,... | collective-permute-start | bytes 798728 | tf_op jit(solution)/shard_map/ppermute | solution.py:496
  5.0 0.1 collective-permute-start.2
  5.1 3.6 %collective-permute-start.3 = (f32[65,8,128]{2,1,0:T(8,128)}, f32[65,8,128]{2,1,0:T(8,128)S(1)}, u32[]{:S(2)}, u32[]{:S(2)}) collective-permute-start(f32[65,8,128]{2,1,0:T(8,128)} %bitcast.12), channel_id=1, source_target_pairs={{0,4},{4,8},{8,12},{12,16},{16,20},{20,24},{24,28},{1,5},{5,9},{9,... | collective-permute-start | bytes 798728 | tf_op jit(solution)/shard_map/ppermute | solution.py:530
  8.7 1.3 %collective-permute-start.4 = (f32[65,8,128]{2,1,0:T(8,128)}, f32[65,8,128]{2,1,0:T(8,128)S(1)}, u32[]{:S(2)}, u32[]{:S(2)}) collective-permute-start(f32[65,8,128]{2,1,0:T(8,128)} %bitcast.13), channel_id=1, source_target_pairs={{4,0},{8,4},{12,8},{16,12},{20,16},{24,20},{28,24},{5,1},{9,5},{13... | collective-permute-start | bytes 798728 | tf_op jit(solution)/shard_map/ppermute | solution.py:529
  10.0 0.0 copy-done.3
  10.0 0.0 copy-done.6
  10.1 0.0 copy-done.7
  10.1 0.0 copy-start
  10.1 0.0 copy-start.2
  10.1 0.0 copy-start.4
  10.1 0.0 copy-start.5
  10.1 7.1 %left.1 = (bf16[64,2,144,128]{3,2,1,0:T(8,128)(2,1)S(1)}, s32[2,305]{1,0:T(2,128)S(1)}) custom-call(s32[4,64]{1,0:T(4,128)S(1)} %bitcast.24, s32[1,64]{1,0:T(1,128)S(1)} %bitcast.25, f32[3,64,144]{2,1,0:T(8,128)S(1)} %bitcast.21), custom_call_target="tpu_custom_call" | custom-call | flops 10000000000 | bytes 30000000 | tf_op jit(solution)/shard_map/left/pallas_call | solution.py:228
  17.2 0.0 collective-permute-done.refs_3_
  17.2 0.0 collective-permute-done.1.refs_4_
  17.2 0.5 collective-permute-done.2.refs_5_
  17.8 3.0 %collective-permute-done.3 = f32[65,8,128]{2,1,0:T(8,128)S(1)} collective-permute-done((f32[65,8,128]{2,1,0:T(8,128)}, f32[65,8,128]{2,1,0:T(8,128)S(1)}, u32[]{:S(2)}, u32[]{:S(2)}) %collective-permute-start.3) | collective-permute-done | bytes 266272 | tf_op jit(solution)/shard_map/ppermute | solution.py:530
  20.8 0.0 collective-permute-done.4
  20.9 0.1 collective-permute-start.7
  21.0 1.6 %collective-permute-start.8 = (f32[128,8,128]{2,1,0:T(8,128)S(1)}, f32[128,8,128]{2,1,0:T(8,128)S(1)}, u32[]{:S(2)}, u32[]{:S(2)}) collective-permute-start(f32[128,8,128]{2,1,0:T(8,128)S(1)} %pad_maximum_fusion.refs_2_), channel_id=1, source_target_pairs={{0,2},{1,3},{2,0},{3,1},{4,6},{5,7},{6,4},{7,5},{8,10},{9,11},{10,... | collective-permute-start | bytes 1572872 | tf_op jit(solution)/shard_map/ppermute | solution.py:496
  22.6 0.3 collective-permute-start.9
  22.9 0.0 copy-done
  22.9 2.4 %collective-permute-start.5 = (f32[4,8,128]{2,1,0:T(8,128)S(1)}, f32[4,8,128]{2,1,0:T(8,128)S(1)}, u32[]{:S(2)}, u32[]{:S(2)}) collective-permute-start(f32[4,8,128]{2,1,0:T(8,128)S(1)} %pad_maximum_fusion.3.refs_11_), channel_id=1, source_target_pairs={{0,4},{4,0},{8,12},{12,8},{16,20},{20,16},{24,28},{28,24},{1,5},{5... | collective-permute-start | bytes 49160 | tf_op jit(solution)/shard_map/ppermute | solution.py:496
  25.3 0.0 copy-done.2
  25.3 0.0 copy-done.4
  25.3 0.0 copy-done.5
  25.3 0.0 copy-start.1
  25.4 0.6 setup.1
  26.0 1.1 %collective-permute-done.5.refs_12_ = f32[4,8,128]{2,1,0:T(8,128)S(1)} collective-permute-done((f32[4,8,128]{2,1,0:T(8,128)S(1)}, f32[4,8,128]{2,1,0:T(8,128)S(1)}, u32[]{:S(2)}, u32[]{:S(2)}) %collective-permute-start.5) | collective-permute-done | bytes 16416 | tf_op jit(solution)/shard_map/ppermute | solution.py:496
  27.1 3.0 %collective-permute-start.6 = (f32[8,8,128]{2,1,0:T(8,128)S(1)}, f32[8,8,128]{2,1,0:T(8,128)S(1)}, u32[]{:S(2)}, u32[]{:S(2)}) collective-permute-start(f32[8,8,128]{2,1,0:T(8,128)S(1)} %pad_maximum_fusion.2), channel_id=1, source_target_pairs={{0,8},{4,12},{8,0},{12,4},{16,24},{20,28},{24,16},{28,20},{1,9},{5... | collective-permute-start | bytes 98312 | tf_op jit(solution)/shard_map/ppermute | solution.py:496
  30.1 1.9 %collective-permute-done.6.refs_13_ = f32[8,8,128]{2,1,0:T(8,128)S(1)} collective-permute-done((f32[8,8,128]{2,1,0:T(8,128)S(1)}, f32[8,8,128]{2,1,0:T(8,128)S(1)}, u32[]{:S(2)}, u32[]{:S(2)}) %collective-permute-start.6) | collective-permute-done | bytes 32800 | tf_op jit(solution)/shard_map/ppermute | solution.py:496
  32.0 3.0 %collective-permute-start.10 = (f32[16,8,128]{2,1,0:T(8,128)S(1)}, f32[16,8,128]{2,1,0:T(8,128)S(1)}, u32[]{:S(2)}, u32[]{:S(2)}) collective-permute-start(f32[16,8,128]{2,1,0:T(8,128)S(1)} %pad_maximum_fusion.1), channel_id=1, source_target_pairs={{0,16},{4,20},{8,24},{12,28},{16,0},{20,4},{24,8},{28,12},{1,17},{... | collective-permute-start | bytes 196616 | tf_op jit(solution)/shard_map/ppermute | solution.py:496
  35.0 0.0 copy-done.1
  35.0 24.0 %near_own.1 = (f32[3,144,128]{2,1,0:T(8,128)S(1)}, f32[64,8,128]{2,1,0:T(8,128)S(1)}) custom-call(s32[2,305]{1,0:T(2,128)S(1)} %get-tuple-element.31.refs_0_, f32[3,64]{1,0:T(4,128)S(1)} %bitcast.17, f32[65,8,128]{2,1,0:T(8,128)S(1)} %bitcast.15, f32[65,8,128]{2,1,0:T(8,128)S(1)} %collective-permute-done.refs_3_, ...), custom_call_target="tpu_custom_call" | custom-call | flops 300000000 | bytes 900000 | tf_op jit(solution)/shard_map/near_own/pallas_call | solution.py:445
  59.1 0.0 collective-permute-done.10.refs_14_
  59.1 0.0 collective-permute-done.7.refs_3_
  59.1 0.0 collective-permute-done.8.refs_4_
  59.1 0.0 collective-permute-done.9.refs_5_
  59.1 25.6 %near_last.1 = f32[3,64,144]{2,1,0:T(8,128)} custom-call(s32[2,305]{1,0:T(2,128)S(1)} %get-tuple-element.31.refs_0_, f32[3,64]{1,0:T(4,128)S(1)} %bitcast.18, f32[128,8,128]{2,1,0:T(8,128)S(1)} %pad_maximum_fusion.refs_2_, f32[128,8,128]{2,1,0:T(8,128)S(1)} %collective-permute-done.7.refs_3_, f32[128,8,128]{2,1,0:T(8,128)S(1)} %collective-permute-done.8.refs_4_, ...), custom_call_target="tpu_custom_call" | custom-call | flops 24999999488 | bytes 75000000 | tf_op jit(solution)/shard_map/near_last/pallas_call | solution.py:445
  (10 shorter events, 0.1 us)
Async XLA Ops:
  0.0 10.0 %copy-start.3 = (f32[64,3,144]{2,0,1:T(8,128)S(1)}, f32[64,3,144]{2,0,1:T(8,128)}, u32[]{:S(2)}) copy-start(f32[64,3,144]{2,0,1:T(8,128)} %param.11) | copy-start | bytes 331780
  0.0 10.0 %copy-start.6 = (s32[64,4]{0,1:T(4,128)S(1)}, s32[64,4]{0,1:T(4,128)}, u32[]{:S(2)}) copy-start(s32[64,4]{0,1:T(4,128)} %param.16) | copy-start | bytes 3076
  0.0 10.1 %copy-start.7 = (s32[64]{0:T(128)S(1)}, s32[64]{0:T(128)}, u32[]{:S(2)}) copy-start(s32[64]{0:T(128)} %param.17) | copy-start | bytes 772
  2.0 15.2 %collective-permute-start = (f32[65,8,128]{2,1,0:T(8,128)}, f32[65,8,128]{2,1,0:T(8,128)S(1)}, u32[]{:S(2)}, u32[]{:S(2)}) collective-permute-start(f32[65,8,128]{2,1,0:T(8,128)} %bitcast.9), channel_id=1, source_target_pairs={{0,1},{1,0},{2,3},{3,2},{4,5},{5,4},{6,7},{7,6},{8,9},{9,8},{10,11... | collective-permute-start | bytes 798728 | tf_op jit(solution)/shard_map/ppermute | solution.py:496
  2.5 14.8 %collective-permute-start.1 = (f32[65,8,128]{2,1,0:T(8,128)}, f32[65,8,128]{2,1,0:T(8,128)S(1)}, u32[]{:S(2)}, u32[]{:S(2)}) collective-permute-start(f32[65,8,128]{2,1,0:T(8,128)} %bitcast.10), channel_id=1, source_target_pairs={{0,2},{1,3},{2,0},{3,1},{4,6},{5,7},{6,4},{7,5},{8,10},{9,11},{10,... | collective-permute-start | bytes 798728 | tf_op jit(solution)/shard_map/ppermute | solution.py:496
  5.0 12.8 %collective-permute-start.2 = (f32[65,8,128]{2,1,0:T(8,128)}, f32[65,8,128]{2,1,0:T(8,128)S(1)}, u32[]{:S(2)}, u32[]{:S(2)}) collective-permute-start(f32[65,8,128]{2,1,0:T(8,128)} %bitcast.11), channel_id=1, source_target_pairs={{0,3},{1,2},{2,1},{3,0},{4,7},{5,6},{6,5},{7,4},{8,11},{9,10},{10,... | collective-permute-start | bytes 798728 | tf_op jit(solution)/shard_map/ppermute | solution.py:496
  5.1 15.7 %collective-permute-start.3 = (f32[65,8,128]{2,1,0:T(8,128)}, f32[65,8,128]{2,1,0:T(8,128)S(1)}, u32[]{:S(2)}, u32[]{:S(2)}) collective-permute-start(f32[65,8,128]{2,1,0:T(8,128)} %bitcast.12), channel_id=1, source_target_pairs={{0,4},{4,8},{8,12},{12,16},{16,20},{20,24},{24,28},{1,5},{5,9},{9,... | collective-permute-start | bytes 798728 | tf_op jit(solution)/shard_map/ppermute | solution.py:530
  8.7 12.1 %collective-permute-start.4 = (f32[65,8,128]{2,1,0:T(8,128)}, f32[65,8,128]{2,1,0:T(8,128)S(1)}, u32[]{:S(2)}, u32[]{:S(2)}) collective-permute-start(f32[65,8,128]{2,1,0:T(8,128)} %bitcast.13), channel_id=1, source_target_pairs={{4,0},{8,4},{12,8},{16,12},{20,16},{24,20},{28,24},{5,1},{9,5},{13... | collective-permute-start | bytes 798728 | tf_op jit(solution)/shard_map/ppermute | solution.py:529
  10.1 12.8 %copy-start = (f32[520,128]{1,0:T(8,128)S(1)}, f32[520,128]{1,0:T(8,128)}, u32[]{:S(2)}) copy-start(f32[520,128]{1,0:T(8,128)} %pack.1) | copy-start | bytes 798724
  10.1 15.3 %copy-start.2 = (f32[544,144]{0,1:T(8,128)S(1)}, f32[544,144]{0,1:T(8,128)}, u32[]{:S(2)}) copy-start(f32[544,144]{0,1:T(8,128)} %param.14) | copy-start | bytes 940036
  10.1 15.3 %copy-start.4 = (f32[64,3,144]{2,0,1:T(8,128)S(1)}, f32[64,3,144]{2,0,1:T(8,128)}, u32[]{:S(2)}) copy-start(f32[64,3,144]{2,0,1:T(8,128)} %param.12) | copy-start | bytes 331780
  10.1 15.2 %copy-start.5 = (f32[144,144]{1,0:T(8,128)S(1)}, f32[144,144]{1,0:T(8,128)}, u32[]{:S(2)}) copy-start(f32[144,144]{1,0:T(8,128)} %op_ref.1) | copy-start | bytes 248836
  20.9 38.1 %collective-permute-start.7 = (f32[128,8,128]{2,1,0:T(8,128)S(1)}, f32[128,8,128]{2,1,0:T(8,128)S(1)}, u32[]{:S(2)}, u32[]{:S(2)}) collective-permute-start(f32[128,8,128]{2,1,0:T(8,128)S(1)} %pad_maximum_fusion.refs_2_), channel_id=1, source_target_pairs={{0,1},{1,0},{2,3},{3,2},{4,5},{5,4},{6,7},{7,6},{8,9},{9,8},{10,11... | collective-permute-start | bytes 1572872 | tf_op jit(solution)/shard_map/ppermute | solution.py:496
  21.0 38.1 %collective-permute-start.8 = (f32[128,8,128]{2,1,0:T(8,128)S(1)}, f32[128,8,128]{2,1,0:T(8,128)S(1)}, u32[]{:S(2)}, u32[]{:S(2)}) collective-permute-start(f32[128,8,128]{2,1,0:T(8,128)S(1)} %pad_maximum_fusion.refs_2_), channel_id=1, source_target_pairs={{0,2},{1,3},{2,0},{3,1},{4,6},{5,7},{6,4},{7,5},{8,10},{9,11},{10,... | collective-permute-start | bytes 1572872 | tf_op jit(solution)/shard_map/ppermute | solution.py:496
  22.6 36.5 %collective-permute-start.9 = (f32[128,8,128]{2,1,0:T(8,128)S(1)}, f32[128,8,128]{2,1,0:T(8,128)S(1)}, u32[]{:S(2)}, u32[]{:S(2)}) collective-permute-start(f32[128,8,128]{2,1,0:T(8,128)S(1)} %pad_maximum_fusion.refs_2_), channel_id=1, source_target_pairs={{0,3},{1,2},{2,1},{3,0},{4,7},{5,6},{6,5},{7,4},{8,11},{9,10},{10,... | collective-permute-start | bytes 1572872 | tf_op jit(solution)/shard_map/ppermute | solution.py:496
  22.9 4.2 %collective-permute-start.5 = (f32[4,8,128]{2,1,0:T(8,128)S(1)}, f32[4,8,128]{2,1,0:T(8,128)S(1)}, u32[]{:S(2)}, u32[]{:S(2)}) collective-permute-start(f32[4,8,128]{2,1,0:T(8,128)S(1)} %pad_maximum_fusion.3.refs_11_), channel_id=1, source_target_pairs={{0,4},{4,0},{8,12},{12,8},{16,20},{20,16},{24,28},{28,24},{1,5},{5... | collective-permute-start | bytes 49160 | tf_op jit(solution)/shard_map/ppermute | solution.py:496
  25.3 9.7 %copy-start.1 = (f32[64,3]{0,1:T(4,128)S(1)}, f32[64,3]{0,1:T(4,128)}, u32[]{:S(2)}) copy-start(f32[64,3]{0,1:T(4,128)} %param.10) | copy-start | bytes 2308
  27.1 4.9 %collective-permute-start.6 = (f32[8,8,128]{2,1,0:T(8,128)S(1)}, f32[8,8,128]{2,1,0:T(8,128)S(1)}, u32[]{:S(2)}, u32[]{:S(2)}) collective-permute-start(f32[8,8,128]{2,1,0:T(8,128)S(1)} %pad_maximum_fusion.2), channel_id=1, source_target_pairs={{0,8},{4,12},{8,0},{12,4},{16,24},{20,28},{24,16},{28,20},{1,9},{5... | collective-permute-start | bytes 98312 | tf_op jit(solution)/shard_map/ppermute | solution.py:496
  32.0 27.1 %collective-permute-start.10 = (f32[16,8,128]{2,1,0:T(8,128)S(1)}, f32[16,8,128]{2,1,0:T(8,128)S(1)}, u32[]{:S(2)}, u32[]{:S(2)}) collective-permute-start(f32[16,8,128]{2,1,0:T(8,128)S(1)} %pad_maximum_fusion.1), channel_id=1, source_target_pairs={{0,16},{4,20},{8,24},{12,28},{16,0},{20,4},{24,8},{28,12},{1,17},{... | collective-permute-start | bytes 196616 | tf_op jit(solution)/shard_map/ppermute | solution.py:496
where the time goes:
time: 83.4 us; the launch traced here: 84.7 us
  Pallas kernels  59.4 us (71%)
  starting transfers between devices  18.4 us (22%)
  waiting for transfers between devices  6.59 us (8%)
    pallas_call x2, Pallas kernels, near(): pl.pallas_call(functools.partial(near_kernel, n_blocks, which, last, grou...  49.6 us
    ppermute x9, starting transfers between devices, swap(): lax.ppermute(x, axis, [(i, i ^ bit) for i in range(lax.axis_size(axis))])  13.5 us
    pallas_call x1, Pallas kernels, left(): pl.pallas_call(functools.partial(left_kernel, groups), out_shape=(jax.Sha...  7.1 us
    ppermute x1, starting transfers between devices, shards(): below = lax.ppermute(tiles, 'domain', [(i, i + 1) for i in range(ends)])  3.59 us
    ppermute x9, waiting for transfers between devices, swap(): lax.ppermute(x, axis, [(i, i ^ bit) for i in range(lax.axis_size(axis))])  3.55 us
    ppermute x1, waiting for transfers between devices, shards(): below = lax.ppermute(tiles, 'domain', [(i, i + 1) for i in range(ends)])  3.04 us
    pallas_call x1, Pallas kernels, pack(): pl.pallas_call(pack_kernel, out_shape=jax.ShapeDtypeStruct((8 * rows + 8,...  2.01 us
  transfers between devices with their start and end apart: 11, of which 4 were waited for; matrix products, arithmetic and copies ran while one was open for 0% of the time, Pallas kernels for 37%

commit v1 on v0

--- a/solution.py
+++ b/solution.py
@@ -12,6 +12,7 @@
 UNITS = 8
 BATCH = 32
 TAILS = 16
+LINES = 7
 PADS = BATCH + 2 * UNITS
 HALF = 48
 F32 = jnp.float32
@@ -78,29 +79,28 @@
     lines = []
     for c in range(3):
         grid = off_ref[c] + column(cen_ref[c : c + 1, :])
-        tile_ref[pl.ds(c, rows, 8), :] = grid[:, :128]
+        tile_ref[pl.ds(c, rows, LINES), :] = grid[:, :128]
         tails.append(grid[:, 128:])
     tails.append(jnp.zeros((rows, tail), F32))
     for c in range(3):
         weighted = den_ref[c] * area
-        tile_ref[pl.ds(4 + c, rows, 8), :] = weighted[:, :128]
+        tile_ref[pl.ds(4 + c, rows, LINES), :] = weighted[:, :128]
         tails.append(weighted[:, 128:])
         lines.append(as_row(jnp.sum(weighted, axis=1, keepdims=True)))
     tails.append(jnp.zeros((rows, tail), F32))
-    tile_ref[pl.ds(3, rows, 8), :] = jnp.concatenate(tails, axis=1)
-    tile_ref[pl.ds(7, rows, 8), :] = jnp.zeros((rows, 128), F32)
+    tile_ref[pl.ds(3, rows, LINES), :] = jnp.concatenate(tails, axis=1)
     leaf = (leaf_ref[...] // LEAF_CAP).astype(F32)
     block = jnp.concatenate([cen_ref[...]] + lines + [leaf, jnp.zeros((1, rows), F32)], axis=0)
     lists = list_ref[...].astype(F32)
     rest = 128 - rows - lists.shape[1]
-    tile_ref[8 * rows :, :] = jnp.concatenate([block, lists, jnp.zeros((8, rest), F32)], axis=1)
+    tile_ref[LINES * rows :, :] = jnp.concatenate([block, lists, jnp.zeros((8, rest), F32)], axis=1)
 
 
 def pack(cen, off, den, area, leaf, lists):
     rows = area.shape[0]
     return pl.pallas_call(
         pack_kernel,
-        out_shape=jax.ShapeDtypeStruct((8 * rows + 8, 128), F32),
+        out_shape=jax.ShapeDtypeStruct((LINES * rows + 8, 128), F32),
         in_specs=[VMEM_SPEC] * 6,
         out_specs=VMEM_SPEC,
         compiler_params=params(),
@@ -312,10 +312,10 @@
     rows = left_ref.shape[0]
     points = left_ref.shape[2]
     full = upw_ref.shape[1] - 128
-    held = blocks[0].shape[0] // rows * rows
+    held = blocks[0].shape[0] // (LINES * rows) * (LINES * rows)
     for i, block in enumerate(blocks):
-        pool[pl.ds(i * held, held)] = block[:held]
-    pool[n_blocks * held] = jnp.zeros((8, 128), F32)
+        pool[pl.ds(i * held, held), :] = block[:held, :]
+    pool[pl.ds(n_blocks * held, 16), :] = jnp.zeros((16, 128), F32)
     wa[...] = jnp.zeros_like(wa)
     wb[...] = jnp.zeros_like(wb)
     if last:
@@ -339,7 +339,10 @@
         return [cen_ref[c, t] for c in range(3)]
 
     def upsample(b, _):
-        tiles = [pool[spot_of(list_ref[which, b * BATCH + j])] for j in range(BATCH)]
+        tiles = [
+            pool[pl.ds(LINES * spot_of(list_ref[which, b * BATCH + j]), 8), :]
+            for j in range(BATCH)
+        ]
         heads = jnp.concatenate([jnp.where(body, v, 0.0) for v in tiles], axis=0)
         ends = jnp.concatenate([jnp.where(own_lanes, v[3:4, :], 0.0) for v in tiles], axis=0)
         reach = tail
@@ -433,7 +436,7 @@
         out_shape = (cols, tails)
         out_specs = (VMEM_SPEC, VMEM_SPEC)
     scratch = [
-        pltpu.VMEM((n_blocks * (blocks[0].shape[0] // rows * rows) + 1, 8, 128), F32),
+        pltpu.VMEM((n_blocks * (blocks[0].shape[0] // (LINES * rows) * (LINES * rows)) + 16, 128), F32),
         pltpu.VMEM((size, 8, full), F32),
     ]
     if last:
@@ -524,16 +527,17 @@
     off = jnp.transpose(offsets, (1, 0, 2))
     den = jnp.transpose(density, (1, 0, 2))
     tiles = pack(cen, off, den, area, leaf_slot[None, :], leaf_list)
-    tiles = tiles.reshape(rows + 1, 8, 128)
+    held = LINES * rows
     ends = domains - 1
     above = lax.ppermute(tiles, "domain", [(i + 1, i) for i in range(ends)])
     below = lax.ppermute(tiles, "domain", [(i, i + 1) for i in range(ends)])
     own = by_group(tiles, groups)
 
     lefts, lists = left(groups, near_sources.T, near_counts[None, :], off)
-    own, below, above, den = after((own, below, above, den), (lefts,))
-    both = jnp.concatenate([below[:rows], above[:rows]], axis=0)
-    far = [jnp.concatenate([v[rows:] for v in own], axis=0)]
+    own, den = after((own, den), (lefts,))
+    below, above = after((below, above), (lefts,))
+    both = jnp.concatenate([below[:held], above[:held]], axis=0)
+    far = [jnp.concatenate([v[held:].reshape(1, 8, 128) for v in own], axis=0)]
     hops = []
     steps = bits(domains)
     self_term = None

time: 83.4 us -> 82.9 us (level)
  the two profiles are of different devices: /device:TPU:0 before, /device:TPU:4 now
where the time goes in v1:
time: 82.9 us; the launch traced here: 84.5 us
  Pallas kernels  62 us (75%)
  starting transfers between devices  17 us (21%)
  waiting for transfers between devices  5.22 us (6%)
    pallas_call x2, Pallas kernels, near(): pl.pallas_call(functools.partial(near_kernel, n_blocks, which, last, grou...  52.3 us
    ppermute x9, starting transfers between devices, swap(): lax.ppermute(x, axis, [(i, i ^ bit) for i in range(lax.axis_size(axis))])  12.3 us
    pallas_call x1, Pallas kernels, left(): pl.pallas_call(functools.partial(left_kernel, groups), out_shape=(jax.Sha...  7.09 us
    ppermute x1, starting transfers between devices, shards(): below = lax.ppermute(tiles, 'domain', [(i, i + 1) for i in range(ends)])  3.4 us
    ppermute x9, waiting for transfers between devices, swap(): lax.ppermute(x, axis, [(i, i ^ bit) for i in range(lax.axis_size(axis))])  3.01 us
    ppermute x1, waiting for transfers between devices, shards(): below = lax.ppermute(tiles, 'domain', [(i, i + 1) for i in range(ends)])  2.21 us
    pallas_call x1, Pallas kernels, pack(): pl.pallas_call(pack_kernel, out_shape=jax.ShapeDtypeStruct((LINES * rows...  1.99 us
  transfers between devices with their start and end apart: 11, of which 3 were waited for; matrix products, arithmetic and copies ran while one was open for 0% of the time, Pallas kernels for 41%

profile of v1, /device:TPU:4, one launch (start us, length us, event | category | flops | bytes accessed | tf_op | source)
XLA Modules:
  0.0 84.5 jit_solution(18260465030442139337)
XLA Ops:
  0.0 0.0 copy-start.3
  0.0 0.0 copy-start.6
  0.0 0.0 copy-start.7
  0.0 2.0 %pack.1.refs_2_ = f32[456,128]{1,0:T(8,128)} custom-call(f32[3,64]{1,0:T(4,128)} %bitcast.16, f32[3,64,144]{2,1,0:T(8,128)} %bitcast.20, f32[3,64,144]{2,1,0:T(8,128)} %bitcast.22, f32[64,144]{1,0:T(8,128)} %area_ref.1, s32[1,64]{1,0:T(1,128)} %bitcast.26, s32[8,8]{1,0:T(8,128)} %list_ref.1), custom_call_target="tpu_custom_call" | custom-call | flops 2000000000 | bytes 6000000 | tf_op jit(solution)/shard_map/pack/pallas_call | solution.py:101
  2.0 0.0 collective-permute-start
  2.0 0.0 collective-permute-start.1
  2.0 1.9 %collective-permute-start.2 = (f32[456,128]{1,0:T(8,128)}, f32[456,128]{1,0:T(8,128)S(1)}, u32[]{:S(2)}, u32[]{:S(2)}) collective-permute-start(f32[456,128]{1,0:T(8,128)} %pack.1.refs_2_), channel_id=1, source_target_pairs={{0,3},{1,2},{2,1},{3,0},{4,7},{5,6},{6,5},{7,4},{8,11},{9,10},{10,... | collective-permute-start | bytes 700424 | tf_op jit(solution)/shard_map/ppermute | solution.py:499
  3.9 3.4 %collective-permute-start.5 = (f32[456,128]{1,0:T(8,128)}, f32[456,128]{1,0:T(8,128)S(1)}, u32[]{:S(2)}, u32[]{:S(2)}) collective-permute-start(f32[456,128]{1,0:T(8,128)} %pack.1.refs_2_), channel_id=1, source_target_pairs={{0,4},{4,8},{8,12},{12,16},{16,20},{20,24},{24,28},{1,5},{5,9},{9,... | collective-permute-start | bytes 700424 | tf_op jit(solution)/shard_map/ppermute | solution.py:533
  7.3 1.3 %collective-permute-start.6 = (f32[456,128]{1,0:T(8,128)}, f32[456,128]{1,0:T(8,128)S(1)}, u32[]{:S(2)}, u32[]{:S(2)}) collective-permute-start(f32[456,128]{1,0:T(8,128)} %pack.1.refs_2_), channel_id=1, source_target_pairs={{4,0},{8,4},{12,8},{16,12},{20,16},{24,20},{28,24},{5,1},{9,5},{13... | collective-permute-start | bytes 700424 | tf_op jit(solution)/shard_map/ppermute | solution.py:532
  8.6 0.0 copy-done.3
  8.6 0.0 copy-done.6
  8.6 0.0 copy-done.7
  8.6 0.0 copy-start
  8.6 0.0 copy-start.2
  8.6 0.0 copy-start.4
  8.6 0.0 copy-start.5
  8.6 7.1 %left.1 = (bf16[64,2,144,128]{3,2,1,0:T(8,128)(2,1)S(1)}, s32[2,305]{1,0:T(2,128)S(1)}) custom-call(s32[4,64]{1,0:T(4,128)S(1)} %bitcast.24, s32[1,64]{1,0:T(1,128)S(1)} %bitcast.25, f32[3,64,144]{2,1,0:T(8,128)S(1)} %bitcast.21), custom_call_target="tpu_custom_call" | custom-call | flops 10000000000 | bytes 30000000 | tf_op jit(solution)/shard_map/left/pallas_call | solution.py:228
  15.7 2.2 %collective-permute-done.5 = f32[456,128]{1,0:T(8,128)S(1)} collective-permute-done((f32[456,128]{1,0:T(8,128)}, f32[456,128]{1,0:T(8,128)S(1)}, u32[]{:S(2)}, u32[]{:S(2)}) %collective-permute-start.5) | collective-permute-done | bytes 233504 | tf_op jit(solution)/shard_map/ppermute | solution.py:533
  18.0 0.0 collective-permute-done.6
  18.0 0.1 collective-permute-start.7
  18.1 0.6 collective-permute-start.8
  18.7 0.0 collective-permute-done.refs_3_
  18.7 1.3 %collective-permute-start.9 = (f32[896,128]{1,0:T(8,128)S(1)}, f32[896,128]{1,0:T(8,128)S(1)}, u32[]{:S(2)}, u32[]{:S(2)}) collective-permute-start(f32[896,128]{1,0:T(8,128)S(1)} %pad_maximum_fusion.refs_2_), channel_id=1, source_target_pairs={{0,3},{1,2},{2,1},{3,0},{4,7},{5,6},{6,5},{7,4},{8,11},{9,10},{10,... | collective-permute-start | bytes 1376264 | tf_op jit(solution)/shard_map/ppermute | solution.py:499
  20.0 0.0 collective-permute-done.1.refs_4_
  20.0 0.0 collective-permute-done.2.refs_5_
  20.0 0.0 copy-done
  20.0 2.4 %collective-permute-start.3 = (f32[4,8,128]{2,1,0:T(8,128)S(1)}, f32[4,8,128]{2,1,0:T(8,128)S(1)}, u32[]{:S(2)}, u32[]{:S(2)}) collective-permute-start(f32[4,8,128]{2,1,0:T(8,128)S(1)} %pad_maximum_fusion.3.refs_11_), channel_id=1, source_target_pairs={{0,4},{4,0},{8,12},{12,8},{16,20},{20,16},{24,28},{28,24},{1,5},{5... | collective-permute-start | bytes 49160 | tf_op jit(solution)/shard_map/ppermute | solution.py:499
  22.5 0.0 copy-done.2
  22.5 0.0 copy-done.4
  22.5 0.0 copy-done.5
  22.5 0.0 copy-start.1
  22.5 0.6 setup.1
  23.1 1.1 %collective-permute-done.3.refs_12_ = f32[4,8,128]{2,1,0:T(8,128)S(1)} collective-permute-done((f32[4,8,128]{2,1,0:T(8,128)S(1)}, f32[4,8,128]{2,1,0:T(8,128)S(1)}, u32[]{:S(2)}, u32[]{:S(2)}) %collective-permute-start.3) | collective-permute-done | bytes 16416 | tf_op jit(solution)/shard_map/ppermute | solution.py:499
  24.2 3.0 %collective-permute-start.4 = (f32[8,8,128]{2,1,0:T(8,128)S(1)}, f32[8,8,128]{2,1,0:T(8,128)S(1)}, u32[]{:S(2)}, u32[]{:S(2)}) collective-permute-start(f32[8,8,128]{2,1,0:T(8,128)S(1)} %pad_maximum_fusion.2), channel_id=1, source_target_pairs={{0,8},{4,12},{8,0},{12,4},{16,24},{20,28},{24,16},{28,20},{1,9},{5... | collective-permute-start | bytes 98312 | tf_op jit(solution)/shard_map/ppermute | solution.py:499
  27.2 1.9 %collective-permute-done.4.refs_13_ = f32[8,8,128]{2,1,0:T(8,128)S(1)} collective-permute-done((f32[8,8,128]{2,1,0:T(8,128)S(1)}, f32[8,8,128]{2,1,0:T(8,128)S(1)}, u32[]{:S(2)}, u32[]{:S(2)}) %collective-permute-start.4) | collective-permute-done | bytes 32800 | tf_op jit(solution)/shard_map/ppermute | solution.py:499
  29.1 3.0 %collective-permute-start.10 = (f32[16,8,128]{2,1,0:T(8,128)S(1)}, f32[16,8,128]{2,1,0:T(8,128)S(1)}, u32[]{:S(2)}, u32[]{:S(2)}) collective-permute-start(f32[16,8,128]{2,1,0:T(8,128)S(1)} %pad_maximum_fusion.1), channel_id=1, source_target_pairs={{0,16},{4,20},{8,24},{12,28},{16,0},{20,4},{24,8},{28,12},{1,17},{... | collective-permute-start | bytes 196616 | tf_op jit(solution)/shard_map/ppermute | solution.py:499
  32.1 0.0 copy-done.1
  32.1 26.8 %near_own.1 = (f32[3,144,128]{2,1,0:T(8,128)S(1)}, f32[64,8,128]{2,1,0:T(8,128)S(1)}) custom-call(s32[2,305]{1,0:T(2,128)S(1)} %get-tuple-element.31.refs_0_, f32[3,64]{1,0:T(4,128)S(1)} %bitcast.17, f32[456,128]{1,0:T(8,128)S(1)} %copy-done, f32[456,128]{1,0:T(8,128)S(1)} %collective-permute-done.refs_3_, f32[456,128]{1,0:T(8,128)S(1)} %collective-permute-done.1.refs_4_, ...), custom_call_target="tpu_custom_call" | custom-call | flops 300000000 | bytes 900000 | tf_op jit(solution)/shard_map/near_own/pallas_call | solution.py:448
  58.9 0.0 collective-permute-done.10.refs_14_
  58.9 0.0 collective-permute-done.7.refs_3_
  59.0 0.0 collective-permute-done.8.refs_4_
  59.0 0.0 collective-permute-done.9.refs_5_
  59.0 25.5 %near_last.1 = f32[3,64,144]{2,1,0:T(8,128)} custom-call(s32[2,305]{1,0:T(2,128)S(1)} %get-tuple-element.31.refs_0_, f32[3,64]{1,0:T(4,128)S(1)} %bitcast.18, f32[896,128]{1,0:T(8,128)S(1)} %pad_maximum_fusion.refs_2_, f32[896,128]{1,0:T(8,128)S(1)} %collective-permute-done.7.refs_3_, f32[896,128]{1,0:T(8,128)S(1)} %collective-permute-done.8.refs_4_, ...), custom_call_target="tpu_custom_call" | custom-call | flops 24999999488 | bytes 75000000 | tf_op jit(solution)/shard_map/near_last/pallas_call | solution.py:448
  (8 shorter events, 0.1 us)
Async XLA Ops:
  0.0 8.6 %copy-start.3 = (f32[64,3,144]{2,0,1:T(8,128)S(1)}, f32[64,3,144]{2,0,1:T(8,128)}, u32[]{:S(2)}) copy-start(f32[64,3,144]{2,0,1:T(8,128)} %param.11) | copy-start | bytes 331780
  0.0 8.6 %copy-start.6 = (s32[64,4]{0,1:T(4,128)S(1)}, s32[64,4]{0,1:T(4,128)}, u32[]{:S(2)}) copy-start(s32[64,4]{0,1:T(4,128)} %param.16) | copy-start | bytes 3076
  0.0 8.6 %copy-start.7 = (s32[64]{0:T(128)S(1)}, s32[64]{0:T(128)}, u32[]{:S(2)}) copy-start(s32[64]{0:T(128)} %param.17) | copy-start | bytes 772
  2.0 16.7 %collective-permute-start = (f32[456,128]{1,0:T(8,128)}, f32[456,128]{1,0:T(8,128)S(1)}, u32[]{:S(2)}, u32[]{:S(2)}) collective-permute-start(f32[456,128]{1,0:T(8,128)} %pack.1.refs_2_), channel_id=1, source_target_pairs={{0,1},{1,0},{2,3},{3,2},{4,5},{5,4},{6,7},{7,6},{8,9},{9,8},{10,11... | collective-permute-start | bytes 700424 | tf_op jit(solution)/shard_map/ppermute | solution.py:499
  2.0 18.0 %collective-permute-start.1 = (f32[456,128]{1,0:T(8,128)}, f32[456,128]{1,0:T(8,128)S(1)}, u32[]{:S(2)}, u32[]{:S(2)}) collective-permute-start(f32[456,128]{1,0:T(8,128)} %pack.1.refs_2_), channel_id=1, source_target_pairs={{0,2},{1,3},{2,0},{3,1},{4,6},{5,7},{6,4},{7,5},{8,10},{9,11},{10,... | collective-permute-start | bytes 700424 | tf_op jit(solution)/shard_map/ppermute | solution.py:499
  2.0 18.0 %collective-permute-start.2 = (f32[456,128]{1,0:T(8,128)}, f32[456,128]{1,0:T(8,128)S(1)}, u32[]{:S(2)}, u32[]{:S(2)}) collective-permute-start(f32[456,128]{1,0:T(8,128)} %pack.1.refs_2_), channel_id=1, source_target_pairs={{0,3},{1,2},{2,1},{3,0},{4,7},{5,6},{6,5},{7,4},{8,11},{9,10},{10,... | collective-permute-start | bytes 700424 | tf_op jit(solution)/shard_map/ppermute | solution.py:499
  3.9 14.1 %collective-permute-start.5 = (f32[456,128]{1,0:T(8,128)}, f32[456,128]{1,0:T(8,128)S(1)}, u32[]{:S(2)}, u32[]{:S(2)}) collective-permute-start(f32[456,128]{1,0:T(8,128)} %pack.1.refs_2_), channel_id=1, source_target_pairs={{0,4},{4,8},{8,12},{12,16},{16,20},{20,24},{24,28},{1,5},{5,9},{9,... | collective-permute-start | bytes 700424 | tf_op jit(solution)/shard_map/ppermute | solution.py:533
  7.3 10.7 %collective-permute-start.6 = (f32[456,128]{1,0:T(8,128)}, f32[456,128]{1,0:T(8,128)S(1)}, u32[]{:S(2)}, u32[]{:S(2)}) collective-permute-start(f32[456,128]{1,0:T(8,128)} %pack.1.refs_2_), channel_id=1, source_target_pairs={{4,0},{8,4},{12,8},{16,12},{20,16},{24,20},{28,24},{5,1},{9,5},{13... | collective-permute-start | bytes 700424 | tf_op jit(solution)/shard_map/ppermute | solution.py:532
  8.6 11.4 %copy-start = (f32[456,128]{1,0:T(8,128)S(1)}, f32[456,128]{1,0:T(8,128)}, u32[]{:S(2)}) copy-start(f32[456,128]{1,0:T(8,128)} %pack.1.refs_2_) | copy-start | bytes 700420
  8.6 13.9 %copy-start.2 = (f32[544,144]{0,1:T(8,128)S(1)}, f32[544,144]{0,1:T(8,128)}, u32[]{:S(2)}) copy-start(f32[544,144]{0,1:T(8,128)} %param.14) | copy-start | bytes 940036
  8.6 13.9 %copy-start.4 = (f32[64,3,144]{2,0,1:T(8,128)S(1)}, f32[64,3,144]{2,0,1:T(8,128)}, u32[]{:S(2)}) copy-start(f32[64,3,144]{2,0,1:T(8,128)} %param.12) | copy-start | bytes 331780
  8.6 13.9 %copy-start.5 = (f32[144,144]{1,0:T(8,128)S(1)}, f32[144,144]{1,0:T(8,128)}, u32[]{:S(2)}) copy-start(f32[144,144]{1,0:T(8,128)} %op_ref.1) | copy-start | bytes 248836
  18.0 40.9 %collective-permute-start.7 = (f32[896,128]{1,0:T(8,128)S(1)}, f32[896,128]{1,0:T(8,128)S(1)}, u32[]{:S(2)}, u32[]{:S(2)}) collective-permute-start(f32[896,128]{1,0:T(8,128)S(1)} %pad_maximum_fusion.refs_2_), channel_id=1, source_target_pairs={{0,1},{1,0},{2,3},{3,2},{4,5},{5,4},{6,7},{7,6},{8,9},{9,8},{10,11... | collective-permute-start | bytes 1376264 | tf_op jit(solution)/shard_map/ppermute | solution.py:499
  18.1 40.8 %collective-permute-start.8 = (f32[896,128]{1,0:T(8,128)S(1)}, f32[896,128]{1,0:T(8,128)S(1)}, u32[]{:S(2)}, u32[]{:S(2)}) collective-permute-start(f32[896,128]{1,0:T(8,128)S(1)} %pad_maximum_fusion.refs_2_), channel_id=1, source_target_pairs={{0,2},{1,3},{2,0},{3,1},{4,6},{5,7},{6,4},{7,5},{8,10},{9,11},{10,... | collective-permute-start | bytes 1376264 | tf_op jit(solution)/shard_map/ppermute | solution.py:499
  18.7 40.3 %collective-permute-start.9 = (f32[896,128]{1,0:T(8,128)S(1)}, f32[896,128]{1,0:T(8,128)S(1)}, u32[]{:S(2)}, u32[]{:S(2)}) collective-permute-start(f32[896,128]{1,0:T(8,128)S(1)} %pad_maximum_fusion.refs_2_), channel_id=1, source_target_pairs={{0,3},{1,2},{2,1},{3,0},{4,7},{5,6},{6,5},{7,4},{8,11},{9,10},{10,... | collective-permute-start | bytes 1376264 | tf_op jit(solution)/shard_map/ppermute | solution.py:499
  20.0 4.2 %collective-permute-start.3 = (f32[4,8,128]{2,1,0:T(8,128)S(1)}, f32[4,8,128]{2,1,0:T(8,128)S(1)}, u32[]{:S(2)}, u32[]{:S(2)}) collective-permute-start(f32[4,8,128]{2,1,0:T(8,128)S(1)} %pad_maximum_fusion.3.refs_11_), channel_id=1, source_target_pairs={{0,4},{4,0},{8,12},{12,8},{16,20},{20,16},{24,28},{28,24},{1,5},{5... | collective-permute-start | bytes 49160 | tf_op jit(solution)/shard_map/ppermute | solution.py:499
  22.5 9.7 %copy-start.1 = (f32[64,3]{0,1:T(4,128)S(1)}, f32[64,3]{0,1:T(4,128)}, u32[]{:S(2)}) copy-start(f32[64,3]{0,1:T(4,128)} %param.10) | copy-start | bytes 2308
  24.2 4.9 %collective-permute-start.4 = (f32[8,8,128]{2,1,0:T(8,128)S(1)}, f32[8,8,128]{2,1,0:T(8,128)S(1)}, u32[]{:S(2)}, u32[]{:S(2)}) collective-permute-start(f32[8,8,128]{2,1,0:T(8,128)S(1)} %pad_maximum_fusion.2), channel_id=1, source_target_pairs={{0,8},{4,12},{8,0},{12,4},{16,24},{20,28},{24,16},{28,20},{1,9},{5... | collective-permute-start | bytes 98312 | tf_op jit(solution)/shard_map/ppermute | solution.py:499
  29.1 29.8 %collective-permute-start.10 = (f32[16,8,128]{2,1,0:T(8,128)S(1)}, f32[16,8,128]{2,1,0:T(8,128)S(1)}, u32[]{:S(2)}, u32[]{:S(2)}) collective-permute-start(f32[16,8,128]{2,1,0:T(8,128)S(1)} %pad_maximum_fusion.1), channel_id=1, source_target_pairs={{0,16},{4,20},{8,24},{12,28},{16,0},{20,4},{24,8},{28,12},{1,17},{... | collective-permute-start | bytes 196616 | tf_op jit(solution)/shard_map/ppermute | solution.py:499

commit v2 on v1

--- a/solution.py
+++ b/solution.py
@@ -266,6 +266,13 @@
     for o, part in enumerate(parts):
         h = o % 2
         w[o // 2, h * HALF : (h + 1) * HALF, h * width : (h + 1) * width] = part
+
+
+def clear(w):
+    count, pairs, lines, lanes = w.shape
+    zero = jnp.zeros((count, pairs, lines // 2, lanes // 2), BF16)
+    w[:, :, : lines // 2, lanes // 2 :] = zero
+    w[:, :, lines // 2 :, : lanes // 2] = zero
 
 
 def evaluate(lefts, w, width):
@@ -295,17 +302,15 @@
     return [jnp.sum(s, axis=1, keepdims=True) for s in sums]
 
 
-def near_kernel(n_blocks, which, last, groups, n_far, slots, *refs):
+def near_kernel(n_blocks, which, last, slots, *refs):
     list_ref, cen_ref = refs[:2]
     blocks = refs[2 : 2 + n_blocks]
     refs = refs[2 + n_blocks :]
     left_ref, upw_ref = refs[:2]
     refs = refs[2:]
     if last:
-        cols_in, tail_in, self_ref = refs[:3]
-        far_refs = refs[3 : 3 + n_far]
-        out_ref = refs[3 + n_far]
-        pool, fine, tails, cols, wa, wb, wt = refs[4 + n_far :]
+        cols_in, tail_in, self_ref, far_ref, out_ref = refs[:5]
+        pool, fine, tails, cols, wa, wb, wt = refs[5:]
     else:
         cols, tails, pool, fine, wa, wb = refs
 
@@ -316,10 +321,10 @@
     for i, block in enumerate(blocks):
         pool[pl.ds(i * held, held), :] = block[:held, :]
     pool[pl.ds(n_blocks * held, 16), :] = jnp.zeros((16, 128), F32)
-    wa[...] = jnp.zeros_like(wa)
-    wb[...] = jnp.zeros_like(wb)
+    clear(wa)
+    clear(wb)
     if last:
-        wt[...] = jnp.zeros_like(wt)
+        clear(wt)
         cols[...] = cols_in[...]
         tails[...] = tail_in[...]
     else:
@@ -415,13 +420,12 @@
             return 0
 
         lax.fori_loop(0, rows // TAILS, tail_pass, 0)
-        far = far_sums(groups, rows, far_refs)
         for c in range(3):
             turned = jnp.transpose(cols[c])[:rows]
-            out_ref[c] = turned * (1.0 / EPS) + self_ref[c] + far[c]
-
-
-def near(which, last, groups, blocks, lists, cen, lefts, upw, extra, far=()):
+            out_ref[c] = turned * (1.0 / EPS) + self_ref[c] + far_ref[c][:, :1]
+
+
+def near(which, last, blocks, lists, cen, lefts, upw, extra):
     rows, _, points, _ = lefts.shape
     full = upw.shape[1] - 128
     n_blocks = len(blocks)
@@ -444,9 +448,9 @@
     scratch += [pltpu.VMEM((UNITS, 2, 2 * HALF, 2 * full), BF16)] * 2
     if last:
         scratch += [pltpu.VMEM((TAILS, 2, 2 * HALF, 256), BF16)]
-    n_vmem = n_blocks + 2 + len(extra) + len(far)
+    n_vmem = n_blocks + 2 + len(extra)
     return pl.pallas_call(
-        functools.partial(near_kernel, n_blocks, which, last, groups, len(far), slots),
+        functools.partial(near_kernel, n_blocks, which, last, slots),
         out_shape=out_shape,
         in_specs=[SMEM_SPEC] * 2 + [VMEM_SPEC] * n_vmem,
         out_specs=out_specs,
@@ -454,10 +458,24 @@
         compiler_params=params(44),
         cost_estimate=cost(25 if last else 0.3),
         name="near_last" if last else "near_own",
-    )(lists, cen, *blocks, lefts, upw, *extra, *far)
-
-
-def far_sums(groups, rows, refs):
+    )(lists, cen, *blocks, lefts, upw, *extra)
+
+
+def far_field(groups, rows, loads):
+    return pl.pallas_call(
+        functools.partial(far_kernel, groups),
+        out_shape=jax.ShapeDtypeStruct((3, rows, 128), F32),
+        in_specs=[VMEM_SPEC] * len(loads),
+        out_specs=VMEM_SPEC,
+        compiler_params=params(24),
+        cost_estimate=cost(2),
+        name="far",
+    )(*loads)
+
+
+def far_kernel(groups, *refs):
+    *refs, far_ref = refs
+    rows = far_ref.shape[1]
     domain = lax.axis_index("domain")
     group = lax.axis_index("group")
     block = refs[0][0][:, :rows]
@@ -492,7 +510,8 @@
     sums = [jnp.zeros((rows, 128), F32)] * 3
     for ref in refs:
         sums = lax.fori_loop(0, ref.shape[0] // 2, functools.partial(one, ref), sums, unroll=min(4, ref.shape[0] // 2))
-    return [jnp.sum(v, axis=1, keepdims=True) for v in sums]
+    for c in range(3):
+        far_ref[c] = jnp.broadcast_to(jnp.sum(sums[c], axis=1, keepdims=True), (rows, 128))
 
 
 def swap(x, axis, bit):
@@ -535,25 +554,21 @@
 
     lefts, lists = left(groups, near_sources.T, near_counts[None, :], off)
     own, den = after((own, den), (lefts,))
-    below, above = after((below, above), (lefts,))
+    steps = bits(domains)
+    far = [jnp.concatenate([v[held:].reshape(1, 8, 128) for v in own], axis=0)]
+    far.append(swap(far[0], "domain", steps[0]))
+    below, above = after((below, above), (far,))
     both = jnp.concatenate([below[:held], above[:held]], axis=0)
-    far = [jnp.concatenate([v[held:].reshape(1, 8, 128) for v in own], axis=0)]
-    hops = []
-    steps = bits(domains)
-    self_term = None
-    for turn in range(max(len(steps), groups - 1)):
-        if turn < len(steps):
-            far.append(swap(jnp.concatenate(far, axis=0), "domain", steps[turn]))
-        if turn + 1 < groups:
-            hops.append(swap(both, "group", turn + 1))
-        if turn == 0:
-            self_term, upw = setup(den, self_operator, upsample.T)
-            far = after(far, (self_term,))
-    sides = [both] + hops
+    sides = by_group(both, groups)
+    self_term, upw = setup(den, self_operator, upsample.T)
+    for step in steps[1:]:
+        far.append(swap(jnp.concatenate(far, axis=0), "domain", step))
     lists = after(lists, far[:-1])
-    cols, tails = near(0, False, groups, own, lists, cen, lefts, upw, ())
+    cols, tails = near(0, False, own, lists, cen, lefts, upw, ())
+    far, cols = after((far, cols), (cols,))
     out = near(
-        1, True, groups, sides, lists, cen, lefts, upw, (cols, tails, self_term), far
+        1, True, sides, lists, cen, lefts, upw,
+        (cols, tails, self_term, far_field(groups, rows, far)),
     )
     return jnp.transpose(out, (1, 0, 2))
 

time: 82.9 us -> 79.1 us (0.954)
  the two profiles are of different devices: /device:TPU:4 before, /device:TPU:0 now
where the time goes in v2:
time: 79.1 us; the launch traced here: 78.9 us
  Pallas kernels  58.2 us (74%)
  starting transfers between devices  18.5 us (23%)
  waiting for transfers between devices  1.74 us (2%)
    pallas_call x2, Pallas kernels, near(): pl.pallas_call(functools.partial(near_kernel, n_blocks, which, last, slot...  47 us
    ppermute x9, starting transfers between devices, swap(): lax.ppermute(x, axis, [(i, i ^ bit) for i in range(lax.axis_size(axis))])  13.6 us
    pallas_call x1, Pallas kernels, left(): pl.pallas_call(functools.partial(left_kernel, groups), out_shape=(jax.Sha...  7.1 us
    ppermute x1, starting transfers between devices, shards(): below = lax.ppermute(tiles, 'domain', [(i, i + 1) for i in range(ends)])  3.59 us
    pallas_call x1, Pallas kernels, pack(): pl.pallas_call(pack_kernel, out_shape=jax.ShapeDtypeStruct((LINES * rows...  2 us
    ppermute x9, waiting for transfers between devices, swap(): lax.ppermute(x, axis, [(i, i ^ bit) for i in range(lax.axis_size(axis))])  1.73 us
  transfers between devices with their start and end apart: 11, of which 1 were waited for; matrix products, arithmetic and copies ran while one was open for 0% of the time, Pallas kernels for 45%

profile of v2, /device:TPU:0, one launch (start us, length us, event | category | flops | bytes accessed | tf_op | source)
XLA Modules:
  0.0 78.9 jit_solution(3358216977500155190)
XLA Ops:
  0.0 0.0 copy-start.3
  0.0 0.0 copy-start.6
  0.0 0.0 copy-start.7
  0.0 2.0 %pack.1.refs_2_ = f32[456,128]{1,0:T(8,128)} custom-call(f32[3,64]{1,0:T(4,128)} %bitcast.32, f32[3,64,144]{2,1,0:T(8,128)} %bitcast.36, f32[3,64,144]{2,1,0:T(8,128)} %bitcast.38, f32[64,144]{1,0:T(8,128)} %area_ref.1, s32[1,64]{1,0:T(1,128)} %bitcast.42, s32[8,8]{1,0:T(8,128)} %list_ref.1), custom_call_target="tpu_custom_call" | custom-call | flops 2000000000 | bytes 6000000 | tf_op jit(solution)/shard_map/pack/pallas_call | solution.py:101
  2.0 0.5 collective-permute-start
  2.5 2.5 %collective-permute-start.1 = (f32[456,128]{1,0:T(8,128)}, f32[456,128]{1,0:T(8,128)S(1)}, u32[]{:S(2)}, u32[]{:S(2)}) collective-permute-start(f32[456,128]{1,0:T(8,128)} %pack.1.refs_2_), channel_id=1, source_target_pairs={{0,2},{1,3},{2,0},{3,1},{4,6},{5,7},{6,4},{7,5},{8,10},{9,11},{10,... | collective-permute-start | bytes 700424 | tf_op jit(solution)/shard_map/ppermute | solution.py:518
  5.0 0.1 collective-permute-start.2
  5.1 3.6 %collective-permute-start.5 = (f32[456,128]{1,0:T(8,128)}, f32[456,128]{1,0:T(8,128)S(1)}, u32[]{:S(2)}, u32[]{:S(2)}) collective-permute-start(f32[456,128]{1,0:T(8,128)} %pack.1.refs_2_), channel_id=1, source_target_pairs={{0,4},{4,8},{8,12},{12,16},{16,20},{20,24},{24,28},{1,5},{5,9},{9,... | collective-permute-start | bytes 700424 | tf_op jit(solution)/shard_map/ppermute | solution.py:552
  8.7 1.3 %collective-permute-start.6 = (f32[456,128]{1,0:T(8,128)}, f32[456,128]{1,0:T(8,128)S(1)}, u32[]{:S(2)}, u32[]{:S(2)}) collective-permute-start(f32[456,128]{1,0:T(8,128)} %pack.1.refs_2_), channel_id=1, source_target_pairs={{4,0},{8,4},{12,8},{16,12},{20,16},{24,20},{28,24},{5,1},{9,5},{13... | collective-permute-start | bytes 700424 | tf_op jit(solution)/shard_map/ppermute | solution.py:551
  10.0 0.0 copy-done.3
  10.0 0.0 copy-done.6
  10.0 0.0 copy-done.7
  10.1 0.0 copy-start
  10.1 0.0 copy-start.2
  10.1 0.0 copy-start.4
  10.1 0.0 copy-start.5
  10.1 7.1 %left.1 = (bf16[64,2,144,128]{3,2,1,0:T(8,128)(2,1)S(1)}, s32[2,305]{1,0:T(2,128)S(1)}) custom-call(s32[4,64]{1,0:T(4,128)S(1)} %bitcast.40, s32[1,64]{1,0:T(1,128)S(1)} %bitcast.41, f32[3,64,144]{2,1,0:T(8,128)S(1)} %bitcast.37), custom_call_target="tpu_custom_call" | custom-call | flops 10000000000 | bytes 30000000 | tf_op jit(solution)/shard_map/left/pallas_call | solution.py:228
  17.2 0.0 collective-permute-done.refs_3_
  17.2 0.0 collective-permute-done.1.refs_4_
  17.2 0.0 collective-permute-done.2.refs_5_
  17.2 0.0 copy-done
  17.3 2.7 %collective-permute-start.3 = (f32[4,8,128]{2,1,0:T(8,128)S(1)}, f32[4,8,128]{2,1,0:T(8,128)S(1)}, u32[]{:S(2)}, u32[]{:S(2)}) collective-permute-start(f32[4,8,128]{2,1,0:T(8,128)S(1)} %pad_maximum_fusion.1.refs_0_), channel_id=1, source_target_pairs={{0,4},{4,0},{8,12},{12,8},{16,20},{20,16},{24,28},{28,24},{1,5},{5... | collective-permute-start | bytes 49160 | tf_op jit(solution)/shard_map/ppermute | solution.py:518
  20.0 1.7 %collective-permute-done.3.refs_1_ = f32[4,8,128]{2,1,0:T(8,128)S(1)} collective-permute-done((f32[4,8,128]{2,1,0:T(8,128)S(1)}, f32[4,8,128]{2,1,0:T(8,128)S(1)}, u32[]{:S(2)}, u32[]{:S(2)}) %collective-permute-start.3) | collective-permute-done | bytes 16416 | tf_op jit(solution)/shard_map/ppermute | solution.py:518
  21.7 3.0 %collective-permute-start.4 = (f32[8,8,128]{2,1,0:T(8,128)S(1)}, f32[8,8,128]{2,1,0:T(8,128)S(1)}, u32[]{:S(2)}, u32[]{:S(2)}) collective-permute-start(f32[8,8,128]{2,1,0:T(8,128)S(1)} %get-tuple-element.52), channel_id=1, source_target_pairs={{0,8},{4,12},{8,0},{12,4},{16,24},{20,28},{24,16},{28,20},{1,9},{5... | collective-permute-start | bytes 98312 | tf_op jit(solution)/shard_map/ppermute | solution.py:518
  24.7 0.0 collective-permute-done.5
  24.7 0.0 collective-permute-done.6
  24.8 0.1 collective-permute-start.7
  24.9 1.6 %collective-permute-start.8 = (f32[896,128]{1,0:T(8,128)S(1)}, f32[896,128]{1,0:T(8,128)S(1)}, u32[]{:S(2)}, u32[]{:S(2)}) collective-permute-start(f32[896,128]{1,0:T(8,128)S(1)} %pad_maximum_fusion.refs_2_), channel_id=1, source_target_pairs={{0,2},{1,3},{2,0},{3,1},{4,6},{5,7},{6,4},{7,5},{8,10},{9,11},{10,... | collective-permute-start | bytes 1376264 | tf_op jit(solution)/shard_map/ppermute | solution.py:518
  26.5 0.3 collective-permute-start.9
  26.8 0.0 collective-permute-done.4.refs_2_
  26.8 2.9 %collective-permute-start.10 = (f32[16,8,128]{2,1,0:T(8,128)S(1)}, f32[16,8,128]{2,1,0:T(8,128)S(1)}, u32[]{:S(2)}, u32[]{:S(2)}) collective-permute-start(f32[16,8,128]{2,1,0:T(8,128)S(1)} %constant_dynamic-update-slice_fusion.5), channel_id=1, source_target_pairs={{0,16},{4,20},{8,24},{12,28},{16,0},{20,4},{24,8},{28,12},{1,17},{... | collective-permute-start | bytes 196616 | tf_op jit(solution)/shard_map/ppermute | solution.py:518
  29.6 0.0 copy-done.2
  29.6 0.0 copy-done.4
  29.7 0.0 copy-done.5
  29.7 0.0 copy-start.1
  29.7 0.6 setup.1
  30.3 0.1 copy-done.1
  30.3 26.7 %near_own.1 = (f32[3,144,128]{2,1,0:T(8,128)S(1)}, f32[64,8,128]{2,1,0:T(8,128)S(1)}) custom-call(s32[2,305]{1,0:T(2,128)S(1)} %get-tuple-element.30.refs_0_, f32[3,64]{1,0:T(4,128)S(1)} %bitcast.33, f32[456,128]{1,0:T(8,128)S(1)} %copy-done, f32[456,128]{1,0:T(8,128)S(1)} %collective-permute-done.refs_3_, f32[456,128]{1,0:T(8,128)S(1)} %collective-permute-done.1.refs_4_, ...), custom_call_target="tpu_custom_call" | custom-call | flops 300000000 | bytes 900000 | tf_op jit(solution)/shard_map/near_own/pallas_call | solution.py:452
  57.0 0.0 collective-permute-done.10.refs_3_
  57.1 1.5 %far.1.refs_11_ = f32[3,64,128]{2,1,0:T(8,128)S(1)} custom-call(f32[4,8,128]{2,1,0:T(8,128)S(1)} %pad_maximum_fusion.1.refs_0_, f32[4,8,128]{2,1,0:T(8,128)S(1)} %collective-permute-done.3.refs_1_, f32[8,8,128]{2,1,0:T(8,128)S(1)} %collective-permute-done.4.refs_2_, f32[16,8,128]{2,1,0:T(8,128)S(1)} %collective-permute-done.10.refs_3_), custom_call_target="tpu_custom_call" | custom-call | flops 2000000000 | bytes 6000000 | tf_op jit(solution)/shard_map/far/pallas_call | solution.py:465
  58.5 0.0 collective-permute-done.7.refs_3_
  58.6 0.0 collective-permute-done.8.refs_4_
  58.6 0.0 collective-permute-done.9.refs_5_
  58.6 20.3 %near_last.1 = f32[3,64,144]{2,1,0:T(8,128)} custom-call(s32[2,305]{1,0:T(2,128)S(1)} %get-tuple-element.30.refs_0_, f32[3,64]{1,0:T(4,128)S(1)} %bitcast.34, f32[896,128]{1,0:T(8,128)S(1)} %pad_maximum_fusion.refs_2_, f32[896,128]{1,0:T(8,128)S(1)} %collective-permute-done.7.refs_3_, f32[896,128]{1,0:T(8,128)S(1)} %collective-permute-done.8.refs_4_, ...), custom_call_target="tpu_custom_call" | custom-call | flops 24999999488 | bytes 75000000 | tf_op jit(solution)/shard_map/near_last/pallas_call | solution.py:452
  (12 shorter events, 0.1 us)
Async XLA Ops:
  0.0 10.0 %copy-start.3 = (f32[64,3,144]{2,0,1:T(8,128)S(1)}, f32[64,3,144]{2,0,1:T(8,128)}, u32[]{:S(2)}) copy-start(f32[64,3,144]{2,0,1:T(8,128)} %param.11) | copy-start | bytes 331780
  0.0 10.0 %copy-start.6 = (s32[64,4]{0,1:T(4,128)S(1)}, s32[64,4]{0,1:T(4,128)}, u32[]{:S(2)}) copy-start(s32[64,4]{0,1:T(4,128)} %param.16) | copy-start | bytes 3076
  0.0 10.0 %copy-start.7 = (s32[64]{0:T(128)S(1)}, s32[64]{0:T(128)}, u32[]{:S(2)}) copy-start(s32[64]{0:T(128)} %param.17) | copy-start | bytes 772
  2.0 15.2 %collective-permute-start = (f32[456,128]{1,0:T(8,128)}, f32[456,128]{1,0:T(8,128)S(1)}, u32[]{:S(2)}, u32[]{:S(2)}) collective-permute-start(f32[456,128]{1,0:T(8,128)} %pack.1.refs_2_), channel_id=1, source_target_pairs={{0,1},{1,0},{2,3},{3,2},{4,5},{5,4},{6,7},{7,6},{8,9},{9,8},{10,11... | collective-permute-start | bytes 700424 | tf_op jit(solution)/shard_map/ppermute | solution.py:518
  2.5 14.8 %collective-permute-start.1 = (f32[456,128]{1,0:T(8,128)}, f32[456,128]{1,0:T(8,128)S(1)}, u32[]{:S(2)}, u32[]{:S(2)}) collective-permute-start(f32[456,128]{1,0:T(8,128)} %pack.1.refs_2_), channel_id=1, source_target_pairs={{0,2},{1,3},{2,0},{3,1},{4,6},{5,7},{6,4},{7,5},{8,10},{9,11},{10,... | collective-permute-start | bytes 700424 | tf_op jit(solution)/shard_map/ppermute | solution.py:518
  5.0 12.2 %collective-permute-start.2 = (f32[456,128]{1,0:T(8,128)}, f32[456,128]{1,0:T(8,128)S(1)}, u32[]{:S(2)}, u32[]{:S(2)}) collective-permute-start(f32[456,128]{1,0:T(8,128)} %pack.1.refs_2_), channel_id=1, source_target_pairs={{0,3},{1,2},{2,1},{3,0},{4,7},{5,6},{6,5},{7,4},{8,11},{9,10},{10,... | collective-permute-start | bytes 700424 | tf_op jit(solution)/shard_map/ppermute | solution.py:518
  5.1 19.6 %collective-permute-start.5 = (f32[456,128]{1,0:T(8,128)}, f32[456,128]{1,0:T(8,128)S(1)}, u32[]{:S(2)}, u32[]{:S(2)}) collective-permute-start(f32[456,128]{1,0:T(8,128)} %pack.1.refs_2_), channel_id=1, source_target_pairs={{0,4},{4,8},{8,12},{12,16},{16,20},{20,24},{24,28},{1,5},{5,9},{9,... | collective-permute-start | bytes 700424 | tf_op jit(solution)/shard_map/ppermute | solution.py:552
  8.7 16.0 %collective-permute-start.6 = (f32[456,128]{1,0:T(8,128)}, f32[456,128]{1,0:T(8,128)S(1)}, u32[]{:S(2)}, u32[]{:S(2)}) collective-permute-start(f32[456,128]{1,0:T(8,128)} %pack.1.refs_2_), channel_id=1, source_target_pairs={{4,0},{8,4},{12,8},{16,12},{20,16},{24,20},{28,24},{5,1},{9,5},{13... | collective-permute-start | bytes 700424 | tf_op jit(solution)/shard_map/ppermute | solution.py:551
  10.1 7.2 %copy-start = (f32[456,128]{1,0:T(8,128)S(1)}, f32[456,128]{1,0:T(8,128)}, u32[]{:S(2)}) copy-start(f32[456,128]{1,0:T(8,128)} %pack.1.refs_2_) | copy-start | bytes 700420
  10.1 19.6 %copy-start.2 = (f32[544,144]{0,1:T(8,128)S(1)}, f32[544,144]{0,1:T(8,128)}, u32[]{:S(2)}) copy-start(f32[544,144]{0,1:T(8,128)} %param.14) | copy-start | bytes 940036
  10.1 19.6 %copy-start.4 = (f32[64,3,144]{2,0,1:T(8,128)S(1)}, f32[64,3,144]{2,0,1:T(8,128)}, u32[]{:S(2)}) copy-start(f32[64,3,144]{2,0,1:T(8,128)} %param.12) | copy-start | bytes 331780
  10.1 19.6 %copy-start.5 = (f32[144,144]{1,0:T(8,128)S(1)}, f32[144,144]{1,0:T(8,128)}, u32[]{:S(2)}) copy-start(f32[144,144]{1,0:T(8,128)} %op_ref.1) | copy-start | bytes 248836
  17.3 4.4 %collective-permute-start.3 = (f32[4,8,128]{2,1,0:T(8,128)S(1)}, f32[4,8,128]{2,1,0:T(8,128)S(1)}, u32[]{:S(2)}, u32[]{:S(2)}) collective-permute-start(f32[4,8,128]{2,1,0:T(8,128)S(1)} %pad_maximum_fusion.1.refs_0_), channel_id=1, source_target_pairs={{0,4},{4,0},{8,12},{12,8},{16,20},{20,16},{24,28},{28,24},{1,5},{5... | collective-permute-start | bytes 49160 | tf_op jit(solution)/shard_map/ppermute | solution.py:518
  21.7 5.0 %collective-permute-start.4 = (f32[8,8,128]{2,1,0:T(8,128)S(1)}, f32[8,8,128]{2,1,0:T(8,128)S(1)}, u32[]{:S(2)}, u32[]{:S(2)}) collective-permute-start(f32[8,8,128]{2,1,0:T(8,128)S(1)} %get-tuple-element.52), channel_id=1, source_target_pairs={{0,8},{4,12},{8,0},{12,4},{16,24},{20,28},{24,16},{28,20},{1,9},{5... | collective-permute-start | bytes 98312 | tf_op jit(solution)/shard_map/ppermute | solution.py:518
  24.8 33.7 %collective-permute-start.7 = (f32[896,128]{1,0:T(8,128)S(1)}, f32[896,128]{1,0:T(8,128)S(1)}, u32[]{:S(2)}, u32[]{:S(2)}) collective-permute-start(f32[896,128]{1,0:T(8,128)S(1)} %pad_maximum_fusion.refs_2_), channel_id=1, source_target_pairs={{0,1},{1,0},{2,3},{3,2},{4,5},{5,4},{6,7},{7,6},{8,9},{9,8},{10,11... | collective-permute-start | bytes 1376264 | tf_op jit(solution)/shard_map/ppermute | solution.py:518
  24.9 33.7 %collective-permute-start.8 = (f32[896,128]{1,0:T(8,128)S(1)}, f32[896,128]{1,0:T(8,128)S(1)}, u32[]{:S(2)}, u32[]{:S(2)}) collective-permute-start(f32[896,128]{1,0:T(8,128)S(1)} %pad_maximum_fusion.refs_2_), channel_id=1, source_target_pairs={{0,2},{1,3},{2,0},{3,1},{4,6},{5,7},{6,4},{7,5},{8,10},{9,11},{10,... | collective-permute-start | bytes 1376264 | tf_op jit(solution)/shard_map/ppermute | solution.py:518
  26.5 32.1 %collective-permute-start.9 = (f32[896,128]{1,0:T(8,128)S(1)}, f32[896,128]{1,0:T(8,128)S(1)}, u32[]{:S(2)}, u32[]{:S(2)}) collective-permute-start(f32[896,128]{1,0:T(8,128)S(1)} %pad_maximum_fusion.refs_2_), channel_id=1, source_target_pairs={{0,3},{1,2},{2,1},{3,0},{4,7},{5,6},{6,5},{7,4},{8,11},{9,10},{10,... | collective-permute-start | bytes 1376264 | tf_op jit(solution)/shard_map/ppermute | solution.py:518
  26.8 30.3 %collective-permute-start.10 = (f32[16,8,128]{2,1,0:T(8,128)S(1)}, f32[16,8,128]{2,1,0:T(8,128)S(1)}, u32[]{:S(2)}, u32[]{:S(2)}) collective-permute-start(f32[16,8,128]{2,1,0:T(8,128)S(1)} %constant_dynamic-update-slice_fusion.5), channel_id=1, source_target_pairs={{0,16},{4,20},{8,24},{12,28},{16,0},{20,4},{24,8},{28,12},{1,17},{... | collective-permute-start | bytes 196616 | tf_op jit(solution)/shard_map/ppermute | solution.py:518
  29.7 0.7 copy-start.1
